TPU v7x, 32 devices: a whole 2x2x4 slice. The times are simulated.
32 devices in a mesh: groups: 2 (over x), var: 16 (over z, y, core).
Axes of the slice: x: 2, y: 2, z: 4, core: 2. Of those that a mesh axis runs over, the one named last changes fastest.
Arguments:
- samples: bfloat16 [2048, 57344], P('groups', 'var'), parts along dimension 0, may hold values from -6 to 6
- omega: float32 [4480, 128, 128], P(('groups', 'var')), parts along dimension 0, as said below
- block_rows: int32 [4480], P(('groups', 'var')), parts along dimension 0, may hold values from -1 to 447, as said below
- block_cols: int32 [4480], P(('groups', 'var')), parts along dimension 0, may hold values from -1 to 447, as said below
- block_count: int32 [32], P(('groups', 'var')), parts along dimension 0, may hold values from 28 to 140, as said below
Outputs:
- new_omega: float32 [4480, 128, 128], P(('groups', 'var')), parts along dimension 0
- objective: float32 [2], P('groups'), parts along dimension 0
There are 2 independent parts, one for each index of `groups`. A program takes and returns all parts, laid end to end along the dimension named above; each array names one. Nothing has to cross between parts.
Inputs may be any that keep to these rules, and one draw needn't show every extreme that they name: `block_rows`: the support is symmetric, holds every diagonal block, and every support block lies within 2 column blocks of its column block around the circle of 448 blocks, with the rows wrapping from 447 to 0. The live slots of a device come first and name blocks of its own columns, each block once; slots past the count hold -1. `block_cols`: column block of each live slot, one of the device's own 28 consecutive column blocks; -1 past the count. `block_count`: some device holds 140 live slots. The blocks of omega form a symmetric matrix: the block at (i, j) is the transpose of the block at (j, i). Its diagonal entries lie in 1 to 3. Slots past the count hold zeros.
All inputs are finite; a program needn't handle non-finite values.
Results may differ from a plain program's by a relative error of at most 0.0032.
Values may be sent and summed in bfloat16 or wider, within the bound.
A program may use at most 192 MiB of HBM per device.

v0:
```python
import functools

import jax
import jax.numpy as jnp
from jax import lax
from jax.experimental import pallas as pl
from jax.experimental.pallas import tpu as pltpu
from jax.sharding import PartitionSpec as P

P_SIZE = 57344
BLK = 128
KB = 2
SAMPLES = 1024
WB = 2 * KB + 1
WIN = 6 * BLK
PAIR = 2 * BLK

step_size = 0.5
penalty = 0.1

VMEM = pltpu.VMEM
SMEM = pltpu.SMEM
F32 = jnp.float32
BF16 = jnp.bfloat16


def eye_mask():
    r = lax.broadcasted_iota(jnp.int32, (BLK, BLK), 0)
    c = lax.broadcasted_iota(jnp.int32, (BLK, BLK), 1)
    return r == c


def shrunk(om, g, diagonal):
    moved = om - (step_size * 0.5 / SAMPLES) * g
    bound = step_size * penalty
    if not diagonal:
        return moved - jnp.clip(moved, -bound, bound)
    eye = eye_mask()
    on = moved + step_size / jnp.where(eye, om, 1.0)
    return jnp.where(eye, on, moved - jnp.clip(moved, -bound, bound))


def block_at(ref, row, col):
    return ref[row * BLK : (row + 1) * BLK, col * BLK : (col + 1) * BLK]


def band_products(a, window):
    y = lax.dot_general(a, window, (((1,), (1,)), ((), ())), preferred_element_type=F32)
    b = jnp.dot(y.astype(BF16), window, preferred_element_type=F32)
    return y, b


def fold(v):
    rows, lanes = v.shape
    return jnp.sum(v.reshape(rows // 8, 8, lanes), axis=0)


def interior_kernel(
    cb, slots,
    rows_ref, cols_ref, count_ref, x_hbm, om_hbm,
    out_hbm, inv_ref, edge_ref, al_ref, ar_ref, log_ref, sq_ref, abs_ref,
    x, band, bmat, res, zero, a_buf, x_sem, om_sem, out_sem, zero_sem,
):
    npairs = (cb - 2 * KB + 1) // 2
    nblocks = P_SIZE // BLK
    last = cb - 4

    def x_copy(c):
        at = pl.multiple_of(c * BLK, BLK)
        return pltpu.make_async_copy(
            x_hbm.at[:, pl.ds(at, BLK)], x.at[:, pl.ds(at, BLK)], x_sem.at[c]
        )

    for c in range(min(6, cb)):
        x_copy(c).start()

    def clear(p, _):
        inv_ref[p] = -1
        return 0

    lax.fori_loop(0, cb * WB, clear, 0, unroll=5)
    zero[...] = jnp.zeros_like(zero)

    def load_slot(s, _):
        @pl.when(s < count_ref[0])
        def _():
            col = cols_ref[s]
            diff = rows_ref[s] - col + KB
            diff = jnp.where(diff < 0, diff + nblocks, diff)
            diff = jnp.where(diff >= nblocks, diff - nblocks, diff)
            p = lax.rem(col, cb) * WB + diff
            inv_ref[p] = s
            pltpu.make_async_copy(om_hbm.at[s], band.at[p], om_sem.at[p]).start()

        @pl.when(s >= count_ref[0])
        def _():
            pltpu.make_async_copy(zero, out_hbm.at[s], zero_sem.at[s]).start()

        return 0

    lax.fori_loop(0, slots, load_slot, 0)

    for c in range(6, cb):
        x_copy(c).start()

    log_ref[...] = jnp.zeros_like(log_ref)
    sq_ref[...] = jnp.zeros_like(sq_ref)
    abs_ref[...] = jnp.zeros_like(abs_ref)
    a_buf[...] = jnp.zeros_like(a_buf)

    def prepare(c):
        for d in range(WB):
            p = c * WB + d
            slot = inv_ref[p]

            @pl.when(slot >= 0)
            def _():
                pltpu.make_async_copy(om_hbm.at[0], band.at[p], om_sem.at[p]).wait()

            @pl.when(slot < 0)
            def _():
                band[p] = jnp.zeros((BLK, BLK), F32)

        x_copy(c).wait()

    def tally(c):
        eye = eye_mask()
        total = jnp.zeros((8, BLK), F32)
        for d in range(WB):
            v = jnp.abs(band[c * WB + d])
            total += fold(jnp.where(eye, 0.0, v) if d == KB else v)
        abs_ref[...] += total
        diag = jnp.sum(jnp.where(eye, band[c * WB + KB], 0.0), axis=0, keepdims=True)
        log_ref[0:1, :] += jnp.log(diag)

    for c in range(4):
        prepare(c)
        tally(c)

    def outputs(i, delta):
        j = i - delta
        return j * WB + delta + KB, i * WB + KB - delta

    def finish(r0):
        for a in range(2):
            i = r0 + a
            for delta in range(KB + 1):
                j = i - delta
                low, high = outputs(i, delta)
                g = bmat[i * WB + KB - delta] + bmat[j * WB + KB + delta].T
                res[low] = shrunk(band[low], g, delta == 0)
                if delta:
                    res[high] = shrunk(band[high], g.T, False)

    def out_copies(r0, fresh, act):
        for a in range(2):
            i = r0 + a
            for delta in range(KB + 1):
                ok = i - delta >= KB
                if a == 0 and cb % 2:
                    ok = jnp.logical_and(ok, fresh)
                for p in outputs(i, delta)[: 2 if delta else 1]:
                    slot = inv_ref[p]

                    @pl.when(jnp.logical_and(ok, slot >= 0))
                    def _():
                        act(pltpu.make_async_copy(res.at[p], out_hbm.at[slot], out_sem.at[p]))

    def start_of(k):
        return jnp.minimum(KB + 2 * k, last)

    def step(k, _):
        r0 = start_of(k)
        fresh = r0 == KB + 2 * k
        for extra in range(2):
            c = KB + 2 * k + 2 + extra
            if cb % 2:
                pl.when(c < cb)(lambda: prepare(c))
            else:
                prepare(c)
        before = jnp.maximum(start_of(k - 1), KB)
        finish(before)
        for extra in range(2):
            c = KB + 2 * k + 2 + extra
            if cb % 2:
                pl.when(c < cb)(lambda: tally(c))
            else:
                tally(c)
        for a in range(2):
            for w in range(a, a + WB):
                p = (r0 - 2 + w) * WB + a + 4 - w
                a_buf[a * BLK : (a + 1) * BLK, w * BLK : (w + 1) * BLK] = band[p].astype(BF16)
        window = x[:, pl.ds(pl.multiple_of((r0 - 2) * BLK, BLK), WIN)]
        y, b = band_products(a_buf[...], window)
        square = y * y
        second = fold(square[BLK:])
        first = fold(square[:BLK])
        if cb % 2:
            first = jnp.where(fresh, first, 0.0)
        sq_ref[...] += first + second
        for a in range(2):
            for d in range(WB):
                bmat[(r0 + a) * WB + d] = b[
                    a * BLK : (a + 1) * BLK, (a + d) * BLK : (a + d + 1) * BLK
                ]

        @pl.when(k > 0)
        def _():
            out_copies(before, before == KB + 2 * (k - 1), lambda copy: copy.start())

        return 0

    lax.fori_loop(0, npairs, step, 0)
    finish(start_of(npairs - 1))
    out_copies(
        start_of(npairs - 1),
        start_of(npairs - 1) == KB + 2 * (npairs - 1),
        lambda copy: copy.start(),
    )

    e = cb - 2
    for w, (i, j) in enumerate(((2, 0), (2, 1), (3, 1), (e - 2, e), (e - 1, e), (e - 1, e + 1))):
        edge_ref[w] = bmat[i * WB + j - i + KB]

    for ref, base in ((al_ref, 0), (ar_ref, e)):
        ref[...] = jnp.zeros_like(ref)
        for a in range(2):
            for w in range(a, a + WB):
                j, i = base + a, base - 2 + w
                if 0 <= i < cb:
                    v = band[i * WB + j - i + KB]
                else:
                    v = band[j * WB + i - j + KB].T
                ref[a * BLK : (a + 1) * BLK, w * BLK : (w + 1) * BLK] = v.astype(BF16)

    def drain(k, _):
        r0 = start_of(k)
        out_copies(r0, r0 == KB + 2 * k, lambda copy: copy.wait())
        return 0

    lax.fori_loop(0, npairs, drain, 0)

    def drain_zero(s, _):
        pltpu.make_async_copy(zero, out_hbm.at[s], zero_sem.at[s]).wait()
        return 0

    lax.fori_loop(count_ref[0], slots, drain_zero, 0)


def edge_kernel(
    n, cb,
    x_hbm, hl_hbm, hr_hbm, al, ar, log_in, sq_in, abs_in,
    bl, br, from_left, from_right, sums_out,
    xl, xr, out_l, out_r, in_l, in_r, tile, tiles, load_sem, send_sem, recv_sem, tsend, trecv,
):
    me = lax.axis_index("var")
    right, left = lax.rem(me + 1, n), lax.rem(me + n - 1, n)
    barrier = pltpu.get_barrier_semaphore()

    def greet(k, _):
        pl.semaphore_signal(
            barrier, inc=1, device_id={"var": lax.rem(me + k, n)},
            device_id_type=pl.DeviceIdType.MESH,
        )
        return 0

    lax.fori_loop(1, n, greet, 0)
    width = cb * BLK
    loads = [
        pltpu.make_async_copy(src, dst, load_sem.at[k])
        for k, (src, dst) in enumerate(
            (
                (hl_hbm, xl.at[:, 0:PAIR]),
                (x_hbm.at[:, 0 : 2 * PAIR], xl.at[:, PAIR:WIN]),
                (x_hbm.at[:, width - 2 * PAIR : width], xr.at[:, 0 : 2 * PAIR]),
                (hr_hbm, xr.at[:, 2 * PAIR : WIN]),
            )
        )
    ]
    for load in loads:
        load.start()
    loads[0].wait()
    loads[1].wait()
    y, b = band_products(al[...], xl[...])
    square = fold(y * y)
    bl[...] = b
    for w, (row, col) in enumerate(((0, 0), (0, 1), (1, 1))):
        out_l[w] = block_at(b, row, col).astype(BF16)
    loads[2].wait()
    loads[3].wait()
    y, b = band_products(ar[...], xr[...])
    square = square + fold(y * y) + sq_in[...]
    br[...] = b
    for w, (row, col) in enumerate(((0, 4), (1, 4), (1, 5))):
        out_r[w] = block_at(b, row, col).astype(BF16)

    lanes = square[:, 0:BLK]
    for k in range(1, SAMPLES // BLK):
        lanes = lanes + square[:, k * BLK : (k + 1) * BLK]
    tile[...] = jnp.zeros_like(tile)
    tile[0:1, :] = jnp.sum(log_in[...], axis=0, keepdims=True)
    tile[1:2, :] = jnp.sum(lanes, axis=0, keepdims=True)
    tile[2:3, :] = jnp.sum(abs_in[...], axis=0, keepdims=True)

    pl.semaphore_wait(barrier, n - 1)
    to_left = pltpu.make_async_remote_copy(
        src_ref=out_l, dst_ref=in_r, send_sem=send_sem.at[0], recv_sem=recv_sem.at[0],
        device_id={"var": left}, device_id_type=pl.DeviceIdType.MESH,
    )
    to_right = pltpu.make_async_remote_copy(
        src_ref=out_r, dst_ref=in_l, send_sem=send_sem.at[1], recv_sem=recv_sem.at[1],
        device_id={"var": right}, device_id_type=pl.DeviceIdType.MESH,
    )
    to_left.start()
    to_right.start()

    def tile_copy(k):
        return pltpu.make_async_remote_copy(
            src_ref=tile, dst_ref=tiles.at[k], send_sem=tsend.at[k], recv_sem=trecv.at[k],
            device_id={"var": lax.rem(me + k, n)}, device_id_type=pl.DeviceIdType.MESH,
        )

    def send_tile(k, _):
        tile_copy(k).start()
        return 0

    lax.fori_loop(1, n, send_tile, 0)

    def wait_tile(k, _):
        tile_copy(k).wait()
        return 0

    lax.fori_loop(1, n, wait_tile, 0)
    total = tile[...]
    for k in range(1, n):
        total = total + tiles[k]
    sums_out[...] = total
    to_left.wait()
    to_right.wait()
    from_left[...] = in_l[...]
    from_right[...] = in_r[...]


def finish_kernel(
    cb,
    inv_ref, sums, bl, br, edge, from_left, from_right, om_hbm, out_in,
    out_hbm, obj_ref,
    om, res, om_sem, out_sem,
):
    del out_in
    e = cb - 2
    pairs = [(0, 0), (0, 1), (1, 1), (0, 2), (1, 2), (1, 3), (-2, 0), (-1, 0), (-1, 1)]
    pairs += [(e, e), (e, e + 1), (e + 1, e + 1), (e - 2, e), (e - 1, e), (e - 1, e + 1)]
    pairs += [(e, e + 2), (e + 1, e + 2), (e + 1, e + 3)]
    left_in = {(-2, 0): 0, (-1, 0): 1, (-1, 1): 2}
    right_in = {(e + 2, e): 0, (e + 2, e + 1): 1, (e + 3, e + 1): 2}
    inner = {(2, 0): 0, (2, 1): 1, (3, 1): 2, (e - 2, e): 3, (e - 1, e): 4, (e - 1, e + 1): 5}

    def term(i, j):
        if (i, j) in left_in:
            return from_left[left_in[i, j]].astype(F32)
        if (i, j) in right_in:
            return from_right[right_in[i, j]].astype(F32)
        if (i, j) in inner:
            return edge[inner[i, j]]
        if i in (0, 1):
            return block_at(bl, i, j + 2)
        return block_at(br, i - e, j - e + 2)

    writes = []
    for i, j in pairs:
        if 0 <= j < cb:
            writes.append((i, j))
        if i != j and 0 <= i < cb:
            writes.append((j, i))
    index = {key: w for w, key in enumerate(writes)}
    slot_of = [inv_ref[j * WB + i - j + KB] for i, j in writes]

    def load(w):
        return pltpu.make_async_copy(om_hbm.at[jnp.maximum(slot_of[w], 0)], om.at[w], om_sem.at[w])

    def store(w):
        return pltpu.make_async_copy(res.at[w], out_hbm.at[slot_of[w]], out_sem.at[w])

    for w in range(len(writes)):
        load(w).start()
    lane = jnp.sum(sums[...], axis=1, keepdims=True)
    log_sum, square_sum, abs_sum = lane[0:1, :], lane[1:2, :], lane[2:3, :]
    value = (-log_sum + square_sum / (2.0 * SAMPLES) + penalty * abs_sum) / P_SIZE
    obj_ref[0] = jnp.sum(value)
    for w in range(len(writes)):
        load(w).wait()
    for i, j in pairs:
        g = term(i, j) + term(j, i).T
        if (i, j) in index:
            w = index[i, j]
            res[w] = shrunk(om[w], g, i == j)
        if i != j and (j, i) in index:
            w = index[j, i]
            res[w] = shrunk(om[w], g.T, False)
    for w in range(len(writes)):
        pl.when(slot_of[w] >= 0)(lambda: store(w).start())
    for w in range(len(writes)):
        pl.when(slot_of[w] >= 0)(lambda: store(w).wait())


def on_device(samples, omega, block_rows, block_cols, block_count):
    n = lax.axis_size("var")
    count, width = samples.shape
    cb = width // BLK
    slots = omega.shape[0]
    whole = pl.BlockSpec(memory_space=VMEM)
    scalar = pl.BlockSpec(memory_space=SMEM)
    anywhere = pl.BlockSpec(memory_space=pl.ANY)

    def shape(dims, kind=F32):
        return jax.ShapeDtypeStruct(dims, kind)

    halo_left = lax.ppermute(
        samples[:, width - PAIR :], "var", [(i, (i + 1) % n) for i in range(n)]
    )
    halo_right = lax.ppermute(
        samples[:, :PAIR], "var", [((i + 1) % n, i) for i in range(n)]
    )

    out, inv, edge, al, ar, logs, squares, sizes = pl.pallas_call(
        functools.partial(interior_kernel, cb, slots),
        out_shape=(
            shape((slots, BLK, BLK)), shape((cb * WB,), jnp.int32), shape((6, BLK, BLK)),
            shape((PAIR, WIN), BF16), shape((PAIR, WIN), BF16),
            shape((8, BLK)), shape((8, count)), shape((8, BLK)),
        ),
        in_specs=[scalar, scalar, scalar, anywhere, anywhere],
        out_specs=(anywhere, scalar, whole, whole, whole, whole, whole, whole),
        scratch_shapes=[
            VMEM((count, width), BF16),
            VMEM((cb * WB, BLK, BLK), F32),
            VMEM((cb * WB, BLK, BLK), F32),
            VMEM((cb * WB, BLK, BLK), F32),
            VMEM((BLK, BLK), F32),
            VMEM((PAIR, WIN), BF16),
            pltpu.SemaphoreType.DMA((cb,)),
            pltpu.SemaphoreType.DMA((cb * WB,)),
            pltpu.SemaphoreType.DMA((cb * WB,)),
            pltpu.SemaphoreType.DMA((slots,)),
        ],
        cost_estimate=pl.CostEstimate(
            flops=4 * cb * count * BLK * WIN,
            bytes_accessed=2 * count * width + 8 * slots * BLK * BLK,
            transcendentals=width,
        ),
        compiler_params=pltpu.CompilerParams(vmem_limit_bytes=50 * 2**20),
        name="interior",
    )(block_rows, block_cols, block_count, samples, omega)

    bl, br, from_left, from_right, sums = pl.pallas_call(
        functools.partial(edge_kernel, n, cb),
        out_shape=(
            shape((PAIR, WIN)), shape((PAIR, WIN)),
            shape((3, BLK, BLK), BF16), shape((3, BLK, BLK), BF16), shape((8, BLK)),
        ),
        in_specs=[anywhere] * 3 + [whole] * 5,
        out_specs=(whole,) * 5,
        scratch_shapes=[
            VMEM((count, WIN), BF16),
            VMEM((count, WIN), BF16),
            VMEM((3, BLK, BLK), BF16),
            VMEM((3, BLK, BLK), BF16),
            VMEM((3, BLK, BLK), BF16),
            VMEM((3, BLK, BLK), BF16),
            VMEM((8, BLK), F32),
            VMEM((n, 8, BLK), F32),
            pltpu.SemaphoreType.DMA((4,)),
            pltpu.SemaphoreType.DMA((2,)),
            pltpu.SemaphoreType.DMA((2,)),
            pltpu.SemaphoreType.DMA((n,)),
            pltpu.SemaphoreType.DMA((n,)),
        ],
        cost_estimate=pl.CostEstimate(
            flops=8 * count * PAIR * WIN, bytes_accessed=8 * count * WIN, transcendentals=0
        ),
        compiler_params=pltpu.CompilerParams(
            collective_id=0, has_side_effects=True, vmem_limit_bytes=40 * 2**20
        ),
        name="edges",
    )(samples, halo_left, halo_right, al, ar, logs, squares, sizes)

    new_omega, objective = pl.pallas_call(
        functools.partial(finish_kernel, cb),
        out_shape=(shape((slots, BLK, BLK)), shape((1,))),
        in_specs=[scalar] + [whole] * 6 + [anywhere] * 2,
        out_specs=(anywhere, scalar),
        scratch_shapes=[
            VMEM((26, BLK, BLK), F32),
            VMEM((26, BLK, BLK), F32),
            pltpu.SemaphoreType.DMA((26,)),
            pltpu.SemaphoreType.DMA((26,)),
        ],
        input_output_aliases={8: 0},
        compiler_params=pltpu.CompilerParams(vmem_limit_bytes=40 * 2**20),
        name="outer_blocks",
    )(inv, sums, bl, br, edge, from_left, from_right, omega, out)
    return new_omega, objective


def solution(mesh):
    placed = (
        P("groups", "var"),
        P(("groups", "var"), None, None),
        P(("groups", "var")),
        P(("groups", "var")),
        P(("groups", "var")),
    )
    return jax.shard_map(
        on_device,
        mesh=mesh,
        in_specs=placed,
        out_specs=(P(("groups", "var"), None, None), P("groups")),
        check_vma=False,
    )
```

profile of v0, /device:TPU:0, one launch (start us, length us, event | category | flops | bytes accessed | tf_op | source)
XLA Modules:
  0.0 55.6 jit_solution(16211652780492763787)
XLA Ops:
  0.6 0.0 slice-start
  0.6 1.4 %fusion = (bf16[1024,256]{1,0:T(8,128)(2,1)S(1)}, bf16[1024,256]{1,0:T(8,128)(2,1)S(1)}) fusion(bf16[1024,3584]{1,0:T(8,128)(2,1)} %x_hbm.3), kind=kLoop, calls=%fused_computation | loop fusion | bytes 2097152 | tf_op jit(solution)/shard_map/slice | solution.py:423
  2.1 5.5 %collective-permute-start.1 = (bf16[1024,256]{1,0:T(8,128)(2,1)S(1)}, bf16[1024,256]{1,0:T(8,128)(2,1)S(1)}, u32[]{:S(2)}, u32[]{:S(2)}) collective-permute-start(bf16[1024,256]{1,0:T(8,128)(2,1)S(1)} %get-tuple-element.28), channel_id=1, source_target_pairs={{1,0},{2,1},{3,2},{4,3},{5,4},{6,5},{7,6},{8,7},{9,8},{10,9},{11,1... | collective-permute-start | bytes 1572872 | tf_op jit(solution)/shard_map/ppermute | solution.py:422
  7.6 0.0 collective-permute-start
  8.2 0.0 copy-start.1
  8.2 0.7 %copy-done.1 = s32[140]{0:T(256)S(1)} copy-done((s32[140]{0:T(256)S(1)}, s32[140]{0:T(256)}, u32[]{:S(2)}) %copy-start.1) | copy-done | bytes 584
  8.9 0.0 copy-start.2
  8.9 0.7 %copy-done.2 = s32[140]{0:T(256)S(1)} copy-done((s32[140]{0:T(256)S(1)}, s32[140]{0:T(256)}, u32[]{:S(2)}) %copy-start.2) | copy-done | bytes 584
  9.6 0.0 slice-start.1
  9.6 26.6 %interior.1 = (f32[140,128,128]{2,1,0:T(8,128)}, s32[140]{0:T(256)S(1)}, f32[6,128,128]{2,1,0:T(8,128)S(1)}, bf16[256,768]{1,0:T(8,128)(2,1)S(1)}, bf16[256,768]...) custom-call(s32[140]{0:T(256)S(1)} %copy-done.1, s32[140]{0:T(256)S(1)} %copy-done.2, ...), custom_call_target="tpu_custom_call" | custom-call | flops 11274289152 | bytes 25690112 | tf_op jit(solution)/shard_map/interior/pallas_call | solution.py:426
  36.2 0.0 collective-permute-done.1.hr_hbm
  36.2 0.0 collective-permute-done.hl_hbm
  36.2 0.0 slice-done
  36.2 0.0 slice-done.1
  36.2 10.2 %edges.1 = (f32[256,768]{1,0:T(8,128)S(1)}, f32[256,768]{1,0:T(8,128)S(1)}, bf16[3,128,128]{2,1,0:T(8,128)(2,1)S(1)}, bf16[3,128,128]{2,1,0:T(8,128)(2,1)S(1)}, f32[8,128]{1,0:T(8,128)S(1)}) custom-call(bf16[1024,3584]{1,0:T(8,128)(2,1)S(1)} %bitcast.1, bf16[1024,256]{1,0:T(8,128)(2,1)S(1)} %collective-permute-done.hl_hbm, ...), custom_call_target="tpu_custom_call" | custom-call | flops 1610612736 | bytes 6291456 | tf_op jit(solution)/shard_map/edges/pallas_call | solution.py:456
  46.5 0.0 copy-start
  46.5 3.6 %copy-done = f32[140,128,128]{2,1,0:T(8,128)S(1)} copy-done((f32[140,128,128]{2,1,0:T(8,128)S(1)}, f32[140,128,128]{2,1,0:T(8,128)}, u32[]{:S(2)}) %copy-start) | copy-done | bytes 9175064
  50.1 5.6 %outer_blocks.1 = (f32[140,128,128]{2,1,0:T(8,128)}, f32[1]{0:T(128)}) custom-call(s32[140]{0:T(256)S(1)} %get-tuple-element.15.inv_ref, f32[8,128]{1,0:T(8,128)S(1)} %get-tuple-element.21.sums, f32[256,768]{1,0:T(8,128)S(1)} %get-tuple-element.22.bl, f32[256,768]{1,0:T(8,128)S(1)} %get-tuple-element.23.br, ...), custom_call_target="tpu_custom_call", output_to_operand_aliasing={{0}: (8, {})} | custom-call | tf_op jit(solution)/shard_map/outer_blocks/pallas_call | solution.py:488
  (1 shorter events, 0.0 us)
Async XLA Ops:
  0.6 35.6 %slice-start = ((s8[7340032]{0:T(1024)(128)(4,1)}), s8[4194304]{0:T(1024)(128)(4,1)S(1)}, s32[]{:S(2)}) async-start(s8[7340032]{0:T(1024)(128)(4,1)} %bitcast), calls=%async_computation | async-start | bytes 8388608
  2.1 34.1 %collective-permute-start.1 = (bf16[1024,256]{1,0:T(8,128)(2,1)S(1)}, bf16[1024,256]{1,0:T(8,128)(2,1)S(1)}, u32[]{:S(2)}, u32[]{:S(2)}) collective-permute-start(bf16[1024,256]{1,0:T(8,128)(2,1)S(1)} %get-tuple-element.28), channel_id=1, source_target_pairs={{1,0},{2,1},{3,2},{4,3},{5,4},{6,5},{7,6},{8,7},{9,8},{10,9},{11,1... | collective-permute-start | bytes 1572872 | tf_op jit(solution)/shard_map/ppermute | solution.py:422
  7.6 28.6 %collective-permute-start = (bf16[1024,256]{1,0:T(8,128)(2,1)S(1)}, bf16[1024,256]{1,0:T(8,128)(2,1)S(1)}, u32[]{:S(2)}, u32[]{:S(2)}) collective-permute-start(bf16[1024,256]{1,0:T(8,128)(2,1)S(1)} %get-tuple-element.29), channel_id=1, source_target_pairs={{0,1},{1,2},{2,3},{3,4},{4,5},{5,6},{6,7},{7,8},{8,9},{9,10},{10,1... | collective-permute-start | bytes 1572872 | tf_op jit(solution)/shard_map/ppermute | solution.py:419
  8.2 0.7 %copy-start.1 = (s32[140]{0:T(256)S(1)}, s32[140]{0:T(256)}, u32[]{:S(2)}) copy-start(s32[140]{0:T(256)} %rows_ref.1) | copy-start | bytes 1684
  8.9 0.7 %copy-start.2 = (s32[140]{0:T(256)S(1)}, s32[140]{0:T(256)}, u32[]{:S(2)}) copy-start(s32[140]{0:T(256)} %cols_ref.1) | copy-start | bytes 1684
  9.6 26.6 %slice-start.1 = ((s8[7340032]{0:T(1024)(128)(4,1)}), s8[3145728]{0:T(1024)(128)(4,1)S(1)}, s32[]{:S(2)}) async-start(s8[7340032]{0:T(1024)(128)(4,1)} %bitcast), calls=%async_computation.1 | async-start | bytes 6291456
  46.5 3.6 %copy-start = (f32[140,128,128]{2,1,0:T(8,128)S(1)}, f32[140,128,128]{2,1,0:T(8,128)}, u32[]{:S(2)}) copy-start(f32[140,128,128]{2,1,0:T(8,128)} %om_hbm.3) | copy-start | bytes 27525124
where the time goes:
time: 55.8 us; the launch traced here: 55.6 us
  Pallas kernels  42.4 us (76%)
  local copies, waits for them, and re-layouts  6.39 us (11%)
  starting transfers between devices  5.5 us (10%)
  between operations  1.37 us (2%)
    pallas_call x1, Pallas kernels, on_device(): pl.pallas_call(functools.partial(interior_kernel, cb, slots), out_shape=(...  26.6 us
    pallas_call x1, Pallas kernels, on_device(): pl.pallas_call(functools.partial(edge_kernel, n, cb), out_shape=(shape((P...  10.2 us
    pallas_call x1, Pallas kernels, on_device(): pl.pallas_call(functools.partial(finish_kernel, cb), out_shape=(shape((sl...  5.56 us
    ppermute x1, starting transfers between devices, on_device(): lax.ppermute(samples[:, :PAIR], 'var', [((i + 1) % n, i) for i in range(n)])  5.5 us
    unnamed x10, local copies, waits for them, and re-layouts  4.96 us
    slice x1, local copies, waits for them, and re-layouts, on_device(): samples[:, :PAIR]  1.43 us
  transfers between devices with their start and end apart: 2, of which 0 were waited for; matrix products, arithmetic and copies ran while one was open for 0% of the time, Pallas kernels for 48%

commit v1 on v0

--- a/solution.py
+++ b/solution.py
@@ -50,19 +50,34 @@
     return y, b
 
 
+def outer_pairs(cb):
+    e = cb - 2
+    pairs = [(0, 0), (0, 1), (1, 1), (0, 2), (1, 2), (1, 3), (-2, 0), (-1, 0), (-1, 1)]
+    pairs += [(e, e), (e, e + 1), (e + 1, e + 1), (e - 2, e), (e - 1, e), (e - 1, e + 1)]
+    pairs += [(e, e + 2), (e + 1, e + 2), (e + 1, e + 3)]
+    writes = []
+    for i, j in pairs:
+        if 0 <= j < cb:
+            writes.append((i, j))
+        if i != j and 0 <= i < cb:
+            writes.append((j, i))
+    return pairs, writes
+
+
 def fold(v):
     rows, lanes = v.shape
     return jnp.sum(v.reshape(rows // 8, 8, lanes), axis=0)
 
 
 def interior_kernel(
-    cb, slots,
-    rows_ref, cols_ref, count_ref, x_hbm, om_hbm,
-    out_hbm, inv_ref, edge_ref, al_ref, ar_ref, log_ref, sq_ref, abs_ref,
-    x, band, bmat, res, zero, a_buf, x_sem, om_sem, out_sem, zero_sem,
+    cb, slots, chunk,
+    rows_hbm, cols_hbm, count_ref, x_hbm, om_hbm,
+    out_hbm, inv_ref, edge_ref, om_edge_ref, al_ref, ar_ref, log_ref, sq_ref, abs_ref,
+    rows_ref, cols_ref, ready, x, om, bmat, res, a_buf, tab_sem, x_sem, om_sem, out_sem,
 ):
     npairs = (cb - 2 * KB + 1) // 2
     nblocks = P_SIZE // BLK
+    chunks = slots // chunk
     last = cb - 4
 
     def x_copy(c):
@@ -71,125 +86,159 @@
             x_hbm.at[:, pl.ds(at, BLK)], x.at[:, pl.ds(at, BLK)], x_sem.at[c]
         )
 
-    for c in range(min(6, cb)):
-        x_copy(c).start()
+    def om_copy(m):
+        part = pl.ds(m * chunk, chunk)
+        return pltpu.make_async_copy(om_hbm.at[part], om.at[part], om_sem.at[m])
+
+    def out_copy(m):
+        part = pl.ds(m * chunk, chunk)
+        return pltpu.make_async_copy(res.at[part], out_hbm.at[part], out_sem.at[m])
+
+    tables = [
+        pltpu.make_async_copy(rows_hbm, rows_ref, tab_sem.at[0]),
+        pltpu.make_async_copy(cols_hbm, cols_ref, tab_sem.at[1]),
+    ]
+    for table in tables:
+        table.start()
+    xs = oms = 0
+    while xs < cb or oms < chunks:
+        if oms < chunks:
+            om_copy(oms).start()
+            oms += 1
+        for _ in range(-(-cb // chunks) + (xs == 0)):
+            if xs < cb:
+                x_copy(xs).start()
+                xs += 1
 
     def clear(p, _):
-        inv_ref[p] = -1
-        return 0
-
-    lax.fori_loop(0, cb * WB, clear, 0, unroll=5)
-    zero[...] = jnp.zeros_like(zero)
-
-    def load_slot(s, _):
-        @pl.when(s < count_ref[0])
-        def _():
-            col = cols_ref[s]
-            diff = rows_ref[s] - col + KB
-            diff = jnp.where(diff < 0, diff + nblocks, diff)
-            diff = jnp.where(diff >= nblocks, diff - nblocks, diff)
-            p = lax.rem(col, cb) * WB + diff
-            inv_ref[p] = s
-            pltpu.make_async_copy(om_hbm.at[s], band.at[p], om_sem.at[p]).start()
-
-        @pl.when(s >= count_ref[0])
-        def _():
-            pltpu.make_async_copy(zero, out_hbm.at[s], zero_sem.at[s]).start()
-
-        return 0
-
-    lax.fori_loop(0, slots, load_slot, 0)
-
-    for c in range(6, cb):
-        x_copy(c).start()
-
+        inv_ref[p] = slots
+        return 0
+
+    lax.fori_loop(0, cb * WB + 1, clear, 0, unroll=4)
+    for m in range(chunks):
+        ready[m] = 0
+    om[slots] = jnp.zeros((BLK, BLK), F32)
     log_ref[...] = jnp.zeros_like(log_ref)
     sq_ref[...] = jnp.zeros_like(sq_ref)
     abs_ref[...] = jnp.zeros_like(abs_ref)
     a_buf[...] = jnp.zeros_like(a_buf)
-
-    def prepare(c):
+    count = count_ref[0]
+
+    def no_block(s, _):
+        res[s] = jnp.zeros((BLK, BLK), F32)
+        return 0
+
+    lax.fori_loop(count, slots, no_block, 0)
+    for table in tables:
+        table.wait()
+
+    def place(m, t):
+        s = m * chunk + t
+        col = cols_ref[s]
+        diff = rows_ref[s] - col
+        diff = jnp.where(diff < -KB, diff + nblocks, diff)
+        diff = jnp.where(diff > KB, diff - nblocks, diff)
+        j = lax.rem(col, cb)
+        live = s < count
+        inv_ref[jnp.where(live, j * WB + diff + KB, cb * WB)] = s
+        later = jnp.maximum(j, j + diff)
+        return jnp.where(live, later, 0)
+
+    def place_chunk(m, _):
+        later = place(m, 0)
+        for t in range(1, chunk):
+            later = jnp.maximum(later, place(m, t))
+        done = (later - KB) // 2
+        if cb % 2:
+            done = jnp.where(later >= last, npairs - 1, done)
+        ready[m] = jnp.clip(done, 0, npairs - 1)
+        return 0
+
+    lax.fori_loop(0, chunks, place_chunk, 0)
+
+    def slot_at(i, j):
+        return inv_ref[j * WB + i - j + KB]
+
+    def arrive(c, have):
+        x_copy(c).wait()
+        most = jnp.int32(-1)
         for d in range(WB):
-            p = c * WB + d
-            slot = inv_ref[p]
-
-            @pl.when(slot >= 0)
-            def _():
-                pltpu.make_async_copy(om_hbm.at[0], band.at[p], om_sem.at[p]).wait()
-
-            @pl.when(slot < 0)
-            def _():
-                band[p] = jnp.zeros((BLK, BLK), F32)
-
-        x_copy(c).wait()
+            slot = inv_ref[c * WB + d]
+            most = jnp.maximum(most, jnp.where(slot < slots, slot, -1))
+        upto = (most + chunk) // chunk
+
+        def wait(m, _):
+            om_copy(m).wait()
+            return 0
+
+        lax.fori_loop(have, upto, wait, 0)
+        return jnp.maximum(have, upto)
 
     def tally(c):
         eye = eye_mask()
         total = jnp.zeros((8, BLK), F32)
         for d in range(WB):
-            v = jnp.abs(band[c * WB + d])
-            total += fold(jnp.where(eye, 0.0, v) if d == KB else v)
+            v = om[inv_ref[c * WB + d]]
+            if d == KB:
+                diag = jnp.sum(jnp.where(eye, v, 0.0), axis=0, keepdims=True)
+                v = jnp.where(eye, 0.0, v)
+            total += fold(jnp.abs(v))
         abs_ref[...] += total
-        diag = jnp.sum(jnp.where(eye, band[c * WB + KB], 0.0), axis=0, keepdims=True)
         log_ref[0:1, :] += jnp.log(diag)
 
+    have = jnp.int32(0)
     for c in range(4):
-        prepare(c)
+        have = arrive(c, have)
+    for c in range(4):
         tally(c)
-
-    def outputs(i, delta):
-        j = i - delta
-        return j * WB + delta + KB, i * WB + KB - delta
 
     def finish(r0):
         for a in range(2):
             i = r0 + a
             for delta in range(KB + 1):
                 j = i - delta
-                low, high = outputs(i, delta)
+                low, high = slot_at(i, j), slot_at(j, i)
                 g = bmat[i * WB + KB - delta] + bmat[j * WB + KB + delta].T
-                res[low] = shrunk(band[low], g, delta == 0)
+                res[low] = shrunk(om[low], g, delta == 0)
                 if delta:
-                    res[high] = shrunk(band[high], g.T, False)
-
-    def out_copies(r0, fresh, act):
-        for a in range(2):
-            i = r0 + a
-            for delta in range(KB + 1):
-                ok = i - delta >= KB
-                if a == 0 and cb % 2:
-                    ok = jnp.logical_and(ok, fresh)
-                for p in outputs(i, delta)[: 2 if delta else 1]:
-                    slot = inv_ref[p]
-
-                    @pl.when(jnp.logical_and(ok, slot >= 0))
-                    def _():
-                        act(pltpu.make_async_copy(res.at[p], out_hbm.at[slot], out_sem.at[p]))
+                    res[high] = shrunk(om[high], g.T, False)
 
     def start_of(k):
         return jnp.minimum(KB + 2 * k, last)
 
-    def step(k, _):
+    def send(k, sent):
+        def more(m):
+            return jnp.logical_and(m < chunks, ready[jnp.minimum(m, chunks - 1)] <= k)
+
+        def start(m):
+            out_copy(m).start()
+            return m + 1
+
+        return lax.while_loop(more, start, sent)
+
+    def step(k, carry):
+        have, sent = carry
         r0 = start_of(k)
         fresh = r0 == KB + 2 * k
         for extra in range(2):
             c = KB + 2 * k + 2 + extra
             if cb % 2:
-                pl.when(c < cb)(lambda: prepare(c))
+                have = lax.cond(c < cb, functools.partial(arrive, c), lambda h: h, have)
             else:
-                prepare(c)
+                have = arrive(c, have)
         before = jnp.maximum(start_of(k - 1), KB)
+        for a in range(2):
+            for w in range(a, a + WB):
+                a_buf[a * BLK : (a + 1) * BLK, w * BLK : (w + 1) * BLK] = om[
+                    slot_at(r0 + a, r0 - 2 + w)
+                ].astype(BF16)
         finish(before)
         for extra in range(2):
             c = KB + 2 * k + 2 + extra
             if cb % 2:
-                pl.when(c < cb)(lambda: tally(c))
+                pl.when(c < cb)(functools.partial(tally, c))
             else:
                 tally(c)
-        for a in range(2):
-            for w in range(a, a + WB):
-                p = (r0 - 2 + w) * WB + a + 4 - w
-                a_buf[a * BLK : (a + 1) * BLK, w * BLK : (w + 1) * BLK] = band[p].astype(BF16)
         window = x[:, pl.ds(pl.multiple_of((r0 - 2) * BLK, BLK), WIN)]
         y, b = band_products(a_buf[...], window)
         square = y * y
@@ -203,48 +252,34 @@
                 bmat[(r0 + a) * WB + d] = b[
                     a * BLK : (a + 1) * BLK, (a + d) * BLK : (a + d + 1) * BLK
                 ]
-
-        @pl.when(k > 0)
-        def _():
-            out_copies(before, before == KB + 2 * (k - 1), lambda copy: copy.start())
-
-        return 0
-
-    lax.fori_loop(0, npairs, step, 0)
+        return have, send(k - 1, sent)
+
+    have, sent = lax.fori_loop(0, npairs, step, (have, jnp.int32(0)))
     finish(start_of(npairs - 1))
-    out_copies(
-        start_of(npairs - 1),
-        start_of(npairs - 1) == KB + 2 * (npairs - 1),
-        lambda copy: copy.start(),
-    )
-
+    send(npairs - 1, sent)
+
+    def late(m, _):
+        om_copy(m).wait()
+        return 0
+
+    lax.fori_loop(have, chunks, late, 0)
     e = cb - 2
     for w, (i, j) in enumerate(((2, 0), (2, 1), (3, 1), (e - 2, e), (e - 1, e), (e - 1, e + 1))):
         edge_ref[w] = bmat[i * WB + j - i + KB]
+
+    for w, (i, j) in enumerate(outer_pairs(cb)[1]):
+        om_edge_ref[w] = om[slot_at(i, j)]
 
     for ref, base in ((al_ref, 0), (ar_ref, e)):
         ref[...] = jnp.zeros_like(ref)
         for a in range(2):
             for w in range(a, a + WB):
                 j, i = base + a, base - 2 + w
-                if 0 <= i < cb:
-                    v = band[i * WB + j - i + KB]
-                else:
-                    v = band[j * WB + i - j + KB].T
+                v = om[slot_at(j, i)] if 0 <= i < cb else om[slot_at(i, j)].T
                 ref[a * BLK : (a + 1) * BLK, w * BLK : (w + 1) * BLK] = v.astype(BF16)
 
-    def drain(k, _):
-        r0 = start_of(k)
-        out_copies(r0, r0 == KB + 2 * k, lambda copy: copy.wait())
-        return 0
-
-    lax.fori_loop(0, npairs, drain, 0)
-
-    def drain_zero(s, _):
-        pltpu.make_async_copy(zero, out_hbm.at[s], zero_sem.at[s]).wait()
-        return 0
-
-    lax.fori_loop(count_ref[0], slots, drain_zero, 0)
+    for m in range(chunks):
+        out_copy(m).wait()
 
 
 def edge_kernel(
@@ -342,16 +377,14 @@
 
 
 def finish_kernel(
-    cb,
-    inv_ref, sums, bl, br, edge, from_left, from_right, om_hbm, out_in,
+    cb, slots,
+    inv_ref, sums, bl, br, edge, from_left, from_right, om, out_in,
     out_hbm, obj_ref,
-    om, res, om_sem, out_sem,
+    res, out_sem,
 ):
     del out_in
     e = cb - 2
-    pairs = [(0, 0), (0, 1), (1, 1), (0, 2), (1, 2), (1, 3), (-2, 0), (-1, 0), (-1, 1)]
-    pairs += [(e, e), (e, e + 1), (e + 1, e + 1), (e - 2, e), (e - 1, e), (e - 1, e + 1)]
-    pairs += [(e, e + 2), (e + 1, e + 2), (e + 1, e + 3)]
+    pairs, writes = outer_pairs(cb)
     left_in = {(-2, 0): 0, (-1, 0): 1, (-1, 1): 2}
     right_in = {(e + 2, e): 0, (e + 2, e + 1): 1, (e + 3, e + 1): 2}
     inner = {(2, 0): 0, (2, 1): 1, (3, 1): 2, (e - 2, e): 3, (e - 1, e): 4, (e - 1, e + 1): 5}
@@ -367,29 +400,16 @@
             return block_at(bl, i, j + 2)
         return block_at(br, i - e, j - e + 2)
 
-    writes = []
-    for i, j in pairs:
-        if 0 <= j < cb:
-            writes.append((i, j))
-        if i != j and 0 <= i < cb:
-            writes.append((j, i))
     index = {key: w for w, key in enumerate(writes)}
     slot_of = [inv_ref[j * WB + i - j + KB] for i, j in writes]
 
-    def load(w):
-        return pltpu.make_async_copy(om_hbm.at[jnp.maximum(slot_of[w], 0)], om.at[w], om_sem.at[w])
-
     def store(w):
         return pltpu.make_async_copy(res.at[w], out_hbm.at[slot_of[w]], out_sem.at[w])
 
-    for w in range(len(writes)):
-        load(w).start()
     lane = jnp.sum(sums[...], axis=1, keepdims=True)
     log_sum, square_sum, abs_sum = lane[0:1, :], lane[1:2, :], lane[2:3, :]
     value = (-log_sum + square_sum / (2.0 * SAMPLES) + penalty * abs_sum) / P_SIZE
     obj_ref[0] = jnp.sum(value)
-    for w in range(len(writes)):
-        load(w).wait()
     for i, j in pairs:
         g = term(i, j) + term(j, i).T
         if (i, j) in index:
@@ -399,9 +419,9 @@
             w = index[j, i]
             res[w] = shrunk(om[w], g.T, False)
     for w in range(len(writes)):
-        pl.when(slot_of[w] >= 0)(lambda: store(w).start())
+        pl.when(slot_of[w] < slots)(lambda: store(w).start())
     for w in range(len(writes)):
-        pl.when(slot_of[w] >= 0)(lambda: store(w).wait())
+        pl.when(slot_of[w] < slots)(lambda: store(w).wait())
 
 
 def on_device(samples, omega, block_rows, block_cols, block_count):
@@ -409,9 +429,11 @@
     count, width = samples.shape
     cb = width // BLK
     slots = omega.shape[0]
+    chunk = 2 * WB if slots % (2 * WB) == 0 else WB
     whole = pl.BlockSpec(memory_space=VMEM)
     scalar = pl.BlockSpec(memory_space=SMEM)
     anywhere = pl.BlockSpec(memory_space=pl.ANY)
+    hbm = pl.BlockSpec(memory_space=pltpu.HBM)
 
     def shape(dims, kind=F32):
         return jax.ShapeDtypeStruct(dims, kind)
@@ -423,26 +445,29 @@
         samples[:, :PAIR], "var", [((i + 1) % n, i) for i in range(n)]
     )
 
-    out, inv, edge, al, ar, logs, squares, sizes = pl.pallas_call(
-        functools.partial(interior_kernel, cb, slots),
+    out, inv, edge, omega_edge, al, ar, logs, squares, sizes = pl.pallas_call(
+        functools.partial(interior_kernel, cb, slots, chunk),
         out_shape=(
-            shape((slots, BLK, BLK)), shape((cb * WB,), jnp.int32), shape((6, BLK, BLK)),
+            shape((slots, BLK, BLK)), shape((cb * WB + 1,), jnp.int32), shape((6, BLK, BLK)),
+            shape((26, BLK, BLK)),
             shape((PAIR, WIN), BF16), shape((PAIR, WIN), BF16),
             shape((8, BLK)), shape((8, count)), shape((8, BLK)),
         ),
-        in_specs=[scalar, scalar, scalar, anywhere, anywhere],
-        out_specs=(anywhere, scalar, whole, whole, whole, whole, whole, whole),
+        in_specs=[hbm, hbm, scalar, hbm, hbm],
+        out_specs=(anywhere, scalar) + (whole,) * 7,
         scratch_shapes=[
+            SMEM((slots,), jnp.int32),
+            SMEM((slots,), jnp.int32),
+            SMEM((slots // chunk,), jnp.int32),
             VMEM((count, width), BF16),
+            VMEM((slots + 1, BLK, BLK), F32),
             VMEM((cb * WB, BLK, BLK), F32),
-            VMEM((cb * WB, BLK, BLK), F32),
-            VMEM((cb * WB, BLK, BLK), F32),
-            VMEM((BLK, BLK), F32),
+            VMEM((slots + 1, BLK, BLK), F32),
             VMEM((PAIR, WIN), BF16),
+            pltpu.SemaphoreType.DMA((2,)),
             pltpu.SemaphoreType.DMA((cb,)),
-            pltpu.SemaphoreType.DMA((cb * WB,)),
-            pltpu.SemaphoreType.DMA((cb * WB,)),
-            pltpu.SemaphoreType.DMA((slots,)),
+            pltpu.SemaphoreType.DMA((slots // chunk,)),
+            pltpu.SemaphoreType.DMA((slots // chunk,)),
         ],
         cost_estimate=pl.CostEstimate(
             flops=4 * cb * count * BLK * WIN,
@@ -459,7 +484,7 @@
             shape((PAIR, WIN)), shape((PAIR, WIN)),
             shape((3, BLK, BLK), BF16), shape((3, BLK, BLK), BF16), shape((8, BLK)),
         ),
-        in_specs=[anywhere] * 3 + [whole] * 5,
+        in_specs=[hbm] + [anywhere] * 2 + [whole] * 5,
         out_specs=(whole,) * 5,
         scratch_shapes=[
             VMEM((count, WIN), BF16),
@@ -486,20 +511,18 @@
     )(samples, halo_left, halo_right, al, ar, logs, squares, sizes)
 
     new_omega, objective = pl.pallas_call(
-        functools.partial(finish_kernel, cb),
+        functools.partial(finish_kernel, cb, slots),
         out_shape=(shape((slots, BLK, BLK)), shape((1,))),
-        in_specs=[scalar] + [whole] * 6 + [anywhere] * 2,
+        in_specs=[scalar] + [whole] * 7 + [anywhere],
         out_specs=(anywhere, scalar),
         scratch_shapes=[
             VMEM((26, BLK, BLK), F32),
-            VMEM((26, BLK, BLK), F32),
-            pltpu.SemaphoreType.DMA((26,)),
             pltpu.SemaphoreType.DMA((26,)),
         ],
         input_output_aliases={8: 0},
         compiler_params=pltpu.CompilerParams(vmem_limit_bytes=40 * 2**20),
         name="outer_blocks",
-    )(inv, sums, bl, br, edge, from_left, from_right, omega, out)
+    )(inv, sums, bl, br, edge, from_left, from_right, omega_edge, out)
     return new_omega, objective
 
 

time: 55.8 us -> 45.1 us (0.81)
  Pallas kernels: 42.4 us -> 35.2 us
  local copies, waits for them, and re-layouts: 6.39 us -> 2.79 us
    pallas_call x2, Pallas kernels: 32.1 us -> 24.9 us  [the longest x1 22 us: on_device(): pl.pallas_call(functools.partial(interior_kernel, cb, slots, chunk), out_...]
    unnamed x10 -> x8, local copies, waits for them, and re-layouts: 4.96 us -> 1.36 us
  transfers between devices with their start and end apart: 2 -> 2, of which waited for: 0 -> 0; matrix products, arithmetic and copies ran while one was open for 0% -> 0% of each run, Pallas kernels for 48% -> 49%
where the time goes in v1:
time: 45.1 us; the launch traced here: 44.9 us
  Pallas kernels  35.2 us (78%)
  starting transfers between devices  5.5 us (12%)
  local copies, waits for them, and re-layouts  2.79 us (6%)
  between operations  1.36 us (3%)
    pallas_call x1, Pallas kernels, on_device(): pl.pallas_call(functools.partial(interior_kernel, cb, slots, chunk), out_...  22 us
    pallas_call x1, Pallas kernels, on_device(): pl.pallas_call(functools.partial(edge_kernel, n, cb), out_shape=(shape((P...  10.3 us
    ppermute x1, starting transfers between devices, on_device(): lax.ppermute(samples[:, :PAIR], 'var', [((i + 1) % n, i) for i in range(n)])  5.5 us
    pallas_call x1, Pallas kernels, on_device(): pl.pallas_call(functools.partial(finish_kernel, cb, slots), out_shape=(sh...  2.92 us
    slice x1, local copies, waits for them, and re-layouts, on_device(): samples[:, :PAIR]  1.43 us
    unnamed x8, local copies, waits for them, and re-layouts  1.36 us
  transfers between devices with their start and end apart: 2, of which 0 were waited for; matrix products, arithmetic and copies ran while one was open for 0% of the time, Pallas kernels for 49%

profile of v1, /device:TPU:0, one launch (start us, length us, event | category | flops | bytes accessed | tf_op | source)
XLA Modules:
  0.0 44.9 jit_solution(7271855469550236970)
XLA Ops:
  0.6 0.0 slice-start
  0.6 1.4 %fusion = (bf16[1024,256]{1,0:T(8,128)(2,1)S(1)}, bf16[1024,256]{1,0:T(8,128)(2,1)S(1)}) fusion(bf16[1024,3584]{1,0:T(8,128)(2,1)} %x_hbm.3), kind=kLoop, calls=%fused_computation | loop fusion | bytes 2097152 | tf_op jit(solution)/shard_map/slice | solution.py:445
  2.1 5.5 %collective-permute-start.1 = (bf16[1024,256]{1,0:T(8,128)(2,1)S(1)}, bf16[1024,256]{1,0:T(8,128)(2,1)S(1)}, u32[]{:S(2)}, u32[]{:S(2)}) collective-permute-start(bf16[1024,256]{1,0:T(8,128)(2,1)S(1)} %get-tuple-element.30), channel_id=1, source_target_pairs={{1,0},{2,1},{3,2},{4,3},{5,4},{6,5},{7,6},{8,7},{9,8},{10,9},{11,1... | collective-permute-start | bytes 1572872 | tf_op jit(solution)/shard_map/ppermute | solution.py:444
  7.6 0.0 collective-permute-start
  8.2 0.0 copy-start
  8.2 0.7 %copy-done = s32[140]{0:T(256)S(1)} copy-done((s32[140]{0:T(256)S(1)}, s32[140]{0:T(256)}, u32[]{:S(2)}) %copy-start) | copy-done | bytes 584
  8.9 0.0 copy-start.1
  8.9 0.7 %copy-done.1 = s32[140]{0:T(256)S(1)} copy-done((s32[140]{0:T(256)S(1)}, s32[140]{0:T(256)}, u32[]{:S(2)}) %copy-start.1) | copy-done | bytes 584
  9.6 0.0 slice-start.1
  9.6 22.0 %interior.1 = (f32[140,128,128]{2,1,0:T(8,128)}, s32[141]{0:T(256)S(1)}, f32[6,128,128]{2,1,0:T(8,128)S(1)}, f32[26,128,128]{2,1,0:T(8,128)S(1)}, bf16[256,768]{...) custom-call(s32[140]{0:T(256)S(1)} %copy-done, ...), custom_call_target="tpu_custom_call" | custom-call | flops 11274289152 | bytes 25690112 | tf_op jit(solution)/shard_map/interior/pallas_call | solution.py:448
  31.6 0.0 collective-permute-done.1.hr_hbm
  31.6 0.0 collective-permute-done.hl_hbm
  31.6 0.0 slice-done
  31.6 0.0 slice-done.1
  31.7 10.3 %edges.1 = (f32[256,768]{1,0:T(8,128)S(1)}, f32[256,768]{1,0:T(8,128)S(1)}, bf16[3,128,128]{2,1,0:T(8,128)(2,1)S(1)}, bf16[3,128,128]{2,1,0:T(8,128)(2,1)S(1)}, f32[8,128]{1,0:T(8,128)S(1)}) custom-call(bf16[1024,3584]{1,0:T(8,128)(2,1)S(1)} %bitcast.1, bf16[1024,256]{1,0:T(8,128)(2,1)S(1)} %collective-permute-done.hl_hbm, ...), custom_call_target="tpu_custom_call" | custom-call | flops 1610612736 | bytes 6291456 | tf_op jit(solution)/shard_map/edges/pallas_call | solution.py:481
  42.0 2.9 %outer_blocks.1 = (f32[140,128,128]{2,1,0:T(8,128)}, f32[1]{0:T(128)}) custom-call(s32[141]{0:T(256)S(1)} %get-tuple-element.16.inv_ref, f32[8,128]{1,0:T(8,128)S(1)} %get-tuple-element.22.sums, f32[256,768]{1,0:T(8,128)S(1)} %get-tuple-element.23.bl, f32[256,768]{1,0:T(8,128)S(1)} %get-tuple-element.24.br, ...), custom_call_target="tpu_custom_call", output_to_operand_aliasing={{0}: (8, {})} | custom-call | tf_op jit(solution)/shard_map/outer_blocks/pallas_call | solution.py:513
  (1 shorter events, 0.0 us)
Async XLA Ops:
  0.6 31.0 %slice-start = ((s8[7340032]{0:T(1024)(128)(4,1)}), s8[4194304]{0:T(1024)(128)(4,1)S(1)}, s32[]{:S(2)}) async-start(s8[7340032]{0:T(1024)(128)(4,1)} %bitcast), calls=%async_computation | async-start | bytes 8388608
  2.1 29.5 %collective-permute-start.1 = (bf16[1024,256]{1,0:T(8,128)(2,1)S(1)}, bf16[1024,256]{1,0:T(8,128)(2,1)S(1)}, u32[]{:S(2)}, u32[]{:S(2)}) collective-permute-start(bf16[1024,256]{1,0:T(8,128)(2,1)S(1)} %get-tuple-element.30), channel_id=1, source_target_pairs={{1,0},{2,1},{3,2},{4,3},{5,4},{6,5},{7,6},{8,7},{9,8},{10,9},{11,1... | collective-permute-start | bytes 1572872 | tf_op jit(solution)/shard_map/ppermute | solution.py:444
  7.6 24.1 %collective-permute-start = (bf16[1024,256]{1,0:T(8,128)(2,1)S(1)}, bf16[1024,256]{1,0:T(8,128)(2,1)S(1)}, u32[]{:S(2)}, u32[]{:S(2)}) collective-permute-start(bf16[1024,256]{1,0:T(8,128)(2,1)S(1)} %get-tuple-element.31), channel_id=1, source_target_pairs={{0,1},{1,2},{2,3},{3,4},{4,5},{5,6},{6,7},{7,8},{8,9},{9,10},{10,1... | collective-permute-start | bytes 1572872 | tf_op jit(solution)/shard_map/ppermute | solution.py:441
  8.2 0.7 %copy-start = (s32[140]{0:T(256)S(1)}, s32[140]{0:T(256)}, u32[]{:S(2)}) copy-start(s32[140]{0:T(256)} %rows_hbm.1) | copy-start | bytes 1684
  8.9 0.7 %copy-start.1 = (s32[140]{0:T(256)S(1)}, s32[140]{0:T(256)}, u32[]{:S(2)}) copy-start(s32[140]{0:T(256)} %cols_hbm.1) | copy-start | bytes 1684
  9.6 22.1 %slice-start.1 = ((s8[7340032]{0:T(1024)(128)(4,1)}), s8[3145728]{0:T(1024)(128)(4,1)S(1)}, s32[]{:S(2)}) async-start(s8[7340032]{0:T(1024)(128)(4,1)} %bitcast), calls=%async_computation.1 | async-start | bytes 6291456
